TPU v7x, 256 devices: a whole 4x4x8 slice. The times are simulated.
256 devices in a mesh: frag: 8 (over y, core), band: 32 (over x, z).
Axes of the slice: x: 4, y: 4, z: 8, core: 2. Of those that a mesh axis runs over, the one named last changes fastest.
Arguments:
- wave_coeffs: bfloat16 [8, 256, 262144], P('frag', 'band'), may hold values from -40 to 40
- old_potential: float32 [8, 262144], P('frag'), may hold values from -4 to 4
- occupations: float32 [8, 256], P('frag'), may hold values from 0 to 2
- box_sizes: int32 [8, 3], replicated, may hold values from 32 to 64, as said below
- box_offsets: int32 [8, 3], replicated, may hold values from 0 to 96, as said below
- patch_signs: int32 [8], replicated, may hold values from -1 to 1, as said below
Outputs:
- new_waves: bfloat16 [8, 256, 262144], P('frag', 'band')
- box_potential: float32 [8, 262144], P('frag')
- total_potential: float32 [128, 128, 128], P('band')
Inputs may be any that keep to these rules, and one draw needn't show every extreme that they name: `box_sizes`: each entry is 32, 48 or 64. box_offsets + box_sizes <= 128 in every dimension. `patch_signs`: each entry is -1 or 1.
All inputs are finite; a program needn't handle non-finite values.
Results may differ from a plain program's by a relative error of at most 0.0065.
Values may be sent and summed in bfloat16 or wider, within the bound.
No kernel may reach another device: no remote copies, remote signals or barrier semaphores. Data moves between devices by JAX's collectives and lax.ppermute only.
A program may use at most 192 MiB of HBM per device.

v0:
```python
import functools

import jax
import jax.numpy as jnp
import numpy as np
from jax import lax
from jax.experimental import pallas as pl
from jax.experimental.pallas import tpu as pltpu
from jax.sharding import PartitionSpec as P

NB = 256
BOX = 64
G = 128
NS_ITERS = 8
CELLS = BOX**3
PLANE = BOX * BOX
PEERS = 32
OWN = NB // PEERS
FULL = CELLS // PEERS
EXTRA = FULL // OWN
SIZES, OFFSETS, SIGNS, PLACE = 0, 3, 6, 7
VOLUMES = (8, 12, 16, 18, 24, 27, 32, 36, 48, 64)

step_size = 0.1
screening = 0.5
local_factor = 0.75
epsilon = 1e-06
f32 = jnp.float32
bf16 = jnp.bfloat16


def sine_table():
    index = np.arange(G, dtype=np.float64) + 1.0
    table = np.sqrt(2.0 / (G + 1)) * np.sin(np.pi * index[:, None] * index[None, :] / (G + 1))
    eigen = 2.0 - 2.0 * np.cos(np.pi * index / (G + 1))
    padded = np.zeros((G + BOX, G), np.float32)
    padded[:G] = table
    return padded, eigen.astype(np.float32)


def aligned(offset):
    return pl.multiple_of(offset, 128)


def vmem():
    return pl.BlockSpec(memory_space=pltpu.VMEM)


def smem():
    return pl.BlockSpec(memory_space=pltpu.SMEM)


def box_size(meta):
    f = meta[PLACE, 0]
    return meta[SIZES, f], meta[SIZES + 1, f], meta[SIZES + 2, f]


def box_offset(meta, f):
    return meta[OFFSETS, f], meta[OFFSETS + 1, f], meta[OFFSETS + 2, f]


def params(mib):
    return pltpu.CompilerParams(vmem_limit_bytes=mib * 1024 * 1024)


def runs(total, run, per_dest, carry):
    dest, slot = carry
    places = []
    for _ in range(total // run):
        places.append((dest, slot))
        slot = slot + run
        wrap = slot == per_dest
        dest, slot = jnp.where(wrap, dest + 1, dest), jnp.where(wrap, 0, slot)
    return places, (dest, slot)


def each_part(size, per_dest, deep, body, ready=None):
    sx, sy, sz = size
    run = {64: 4, 32: 2, 48: 1}[deep]

    @pl.when((sz == deep) & (per_dest < VOLUMES[-1]))
    def _():
        def quad(q, carry):
            if ready is not None:
                ready(q + 1)

            def part(g, place):
                places, place = runs(deep // 2, run, per_dest, place)

                def at(plane, i):
                    dest, slot = places[(plane * 8 + i) // run]
                    return dest, aligned((slot + i % run) * 128)

                body(4 * q, g, at)
                return place

            return lax.fori_loop(0, sy // 16, part, carry)

        lax.fori_loop(0, sx // 4, quad, (jnp.int32(0), jnp.int32(0)))


def full_place(q, plane, i):
    flat = i // 8 * 32 + plane * 8 + i % 8
    return 2 * q + flat // 64, flat % 64 * 128


def trial_kernel(meta, wave_in, pot_in, out_ref, kind_ref, held, wave_ref, pot_ref, arrived):
    size = box_size(meta)
    sx, sy, sz = size
    per_dest = (sx * sy * sz) // (PEERS * 128)
    kind = jnp.int32(0)
    for volume in VOLUMES:
        kind = kind + (volume < per_dest).astype(jnp.int32)
    kind_ref[0] = kind
    quads = sx // 4

    def fetch(q):
        lanes = pl.ds(aligned(q * 4 * PLANE), 4 * PLANE)
        wave = pltpu.make_async_copy(wave_in.at[:, lanes], wave_ref.at[:, lanes], arrived.at[0, q])
        return wave, pltpu.make_async_copy(pot_in.at[:, lanes], pot_ref.at[:, lanes], arrived.at[1, q])

    def begin(q, carry):
        for copy in fetch(q):
            copy.start()
        return carry

    def ready(q):
        @pl.when(q < quads)
        def _():
            for copy in fetch(q):
                copy.wait()

    lax.fori_loop(0, quads, begin, 0)
    ready(0)
    lane = lax.broadcasted_iota(jnp.int32, (8, 128), 1)
    z = lane % BOX
    low = lane < BOX
    has_last = (z > 0).astype(f32)
    zero = jnp.zeros((8, 128), f32)

    def load(x, i):
        return wave_ref[:, pl.ds(aligned(x * PLANE + i * 128), 128)].astype(f32)

    def edges(x):
        before = jnp.where(x > 0, 1.0, 0.0)
        after = jnp.where(x + 4 < sx, 1.0, 0.0)
        return before, after, jnp.maximum(x - 1, 0), jnp.minimum(x + 4, sx - 1)

    def stencil(c, turned, last_turned, next_turned, around, has_next, x, i):
        beside = turned + jnp.where(low, last_turned, next_turned)
        beside = beside + (pltpu.roll(c, 127, 1) * has_next + pltpu.roll(c, 1, 1) * has_last)
        beside = beside + around
        pot = pot_ref[:, pl.ds(aligned(x * PLANE + i * 128), 128)]
        return c * ((1.0 - 3.0 * step_size) - step_size * pot) + (0.5 * step_size) * beside

    @pl.when(per_dest == VOLUMES[-1])
    def _():
        has_next = (z < BOX - 1).astype(f32)

        def quad(q, carry):
            ready(q + 1)
            x = 4 * q
            before, after, xb, xa = edges(x)
            last_turned, here = [zero] * 4, [load(x + p, 0) for p in range(4)]
            turned = [pltpu.roll(c, BOX, 1) for c in here]
            for i in range(32):
                ahead = [load(x + p, i + 1) for p in range(4)] if i < 31 else [zero] * 4
                ahead_turned = [pltpu.roll(c, BOX, 1) for c in ahead] if i < 31 else [zero] * 4
                line = [load(xb, i) * before] + here + [load(xa, i) * after]
                for p in range(4):
                    around = line[p] + line[p + 2]
                    value = stencil(here[p], turned[p], last_turned[p], ahead_turned[p], around, has_next, x + p, i)
                    dest, slot = full_place(q, p, i)
                    out_ref[dest, :, slot : slot + 128] = value.astype(bf16)
                here, last_turned, turned = ahead, turned, ahead_turned
            return carry

        lax.fori_loop(0, BOX // 4, quad, 0)

    def some(deep):
        live = (z < deep).astype(f32)
        has_next = (z < deep - 1).astype(f32)

        def part(x, g, at):
            before, after, xb, xa = edges(x)
            top = jnp.where(g > 0, 1.0, 0.0)
            bottom = jnp.where(16 * g + 16 < sy, 1.0, 0.0)
            first, last = jnp.maximum(8 * g - 1, 0), jnp.minimum(8 * g + 8, 31)
            lines = []
            for p in range(4):
                inner = [load(x + p, 8 * g + i) for i in range(8)]
                lines.append([load(x + p, first) * top] + inner + [load(x + p, last) * bottom])
            turned = [[pltpu.roll(c, BOX, 1) for c in line] for line in lines]
            for i in range(8):
                line = [load(xb, 8 * g + i) * before] + [lines[p][i + 1] for p in range(4)] + [load(xa, 8 * g + i) * after]
                for p in range(4):
                    t = turned[p]
                    around = line[p] + line[p + 2]
                    value = stencil(line[p + 1], t[i + 1], t[i], t[i + 2], around, has_next, x + p, 8 * g + i)
                    if deep == BOX:
                        dest, slot = at(p, i)
                        out_ref[dest, :, pl.ds(slot, 128)] = value.astype(bf16)
                    else:
                        held[:, p * 1024 + i * 128 : p * 1024 + (i + 1) * 128] = value * live
            if deep == BOX:
                return

            def kept(p, i):
                return held[:, p * 1024 + i * 128 : p * 1024 + (i + 1) * 128]

            for i in range(8):
                for p in range(deep // 16):
                    if deep == 32:
                        value = kept(2 * p, i) + pltpu.roll(kept(2 * p + 1, i), 32, 1)
                    else:
                        piece = (z >= 16 * p) & (z < 16 * p + 16)
                        value = kept(p, i) + pltpu.roll(jnp.where(piece, kept(3, i), 0.0), 48 - 16 * p, 1)
                    dest, slot = at(p, i)
                    out_ref[dest, :, pl.ds(slot, 128)] = value.astype(bf16)

        each_part(size, per_dest, deep, part, ready)

    for deep in (32, 48, 64):
        some(deep)


def unpack_kernel(meta, in_ref, out_ref):
    size = box_size(meta)
    sx, sy, sz = size
    per_dest = (sx * sy * sz) // (PEERS * 128)
    lane = lax.broadcasted_iota(jnp.int32, (8, 128), 1)
    z = lane % BOX

    def put(x, i, value):
        out_ref[:, pl.ds(aligned(x * PLANE + i * 128), 128)] = value.astype(bf16)

    @pl.when(per_dest == VOLUMES[-1])
    def _():
        def quad(q, carry):
            for i in range(32):
                for p in range(4):
                    dest, slot = full_place(q, p, i)
                    put(4 * q + p, i, in_ref[dest, :, slot : slot + 128])
            return carry

        lax.fori_loop(0, BOX // 4, quad, 0)

    @pl.when(per_dest < VOLUMES[-1])
    def _():
        def clear(i, carry):
            out_ref[:, pl.ds(aligned(i * PLANE), PLANE)] = jnp.zeros((8, PLANE), bf16)
            return carry

        lax.fori_loop(0, BOX, clear, 0)

    def some(deep):
        live = (z < deep).astype(f32)
        gap = (z >= deep).astype(f32)

        def part(x, g, at):
            for i in range(8):
                row = 8 * g + i
                values = []
                for p in range(deep // 16):
                    dest, slot = at(p, i)
                    values.append(in_ref[dest, :, pl.ds(slot, 128)])
                if deep == 64:
                    for p in range(4):
                        put(x + p, row, values[p])
                    continue
                values = [value.astype(f32) for value in values]
                if deep == 32:
                    for p in range(2):
                        put(x + 2 * p, row, values[p] * live)
                        put(x + 2 * p + 1, row, pltpu.roll(values[p], 96, 1) * live)
                else:
                    for p in range(3):
                        put(x + p, row, values[p] * live)
                    rest = [pltpu.roll(values[p] * gap, 80 + 16 * p, 1) for p in range(3)]
                    put(x + 3, row, rest[0] + rest[1] + rest[2])

        each_part(size, per_dest, deep, part)

    for deep in (32, 48, 64):
        some(deep)


def gram_kernel(rows_ref, out_ref, blocks, arrived):
    copies = []
    for i in range(OWN):
        part = rows_ref.at[:, i * EXTRA : (i + 1) * EXTRA]
        copies.append(pltpu.make_async_copy(part, blocks.at[i], arrived.at[i]))
        copies[-1].start()
    total = jnp.zeros((NB, NB), f32)
    for i in range(OWN):
        copies[i].wait()
        block = blocks[i]
        total = total + lax.dot_general(block, block, (((1,), (1,)), ((), ())), preferred_element_type=f32)
    out_ref[...] = total


def halves(value):
    head = value.astype(bf16)
    return head, (value - head.astype(f32)).astype(bf16)


def product(left, right):
    dot = functools.partial(jnp.dot, preferred_element_type=f32)
    return dot(left[0], right[0]) + (dot(left[0], right[1]) + dot(left[1], right[0]))


def newton_kernel(gram_ref, out_ref):
    gram = gram_ref[...] * (1.0 / CELLS)
    frobenius = jnp.sqrt(jnp.sum(gram * gram, keepdims=True) + epsilon)
    row = lax.broadcasted_iota(jnp.int32, (NB, NB), 0)
    column = lax.broadcasted_iota(jnp.int32, (NB, NB), 1)
    three = jnp.where(row == column, 1.5, 0.0)
    square = gram / frobenius
    step = halves(three - 0.5 * square)
    inverse = step
    square = halves(product(halves(square), step))
    for sweep in range(1, NS_ITERS):
        step = halves(three - 0.5 * product(inverse, square))
        if sweep < NS_ITERS - 1:
            square = halves(product(square, step))
        inverse = product(step, inverse)
        if sweep < NS_ITERS - 1:
            inverse = halves(inverse)
    out_ref[...] = (inverse / jnp.sqrt(frobenius)).T.astype(bf16)


def fresh_kernel(coeff_ref, rows_ref, occ_ref, out_ref, blocks, arrived, dens):
    copies = []
    for i in range(OWN):
        part = rows_ref.at[:, i * EXTRA : (i + 1) * EXTRA]
        copies.append(pltpu.make_async_copy(part, blocks.at[i], arrived.at[i]))
        copies[-1].start()
    weight = jnp.broadcast_to(occ_ref[...] * (1.0 / NB), (128, NB)).T[:, 0:1]
    coeff = coeff_ref[...]
    for i in range(OWN):
        copies[i].wait()
        fresh = jnp.dot(coeff, blocks[i], preferred_element_type=f32)
        out_ref[:, i * EXTRA : (i + 1) * EXTRA] = fresh.astype(bf16)
        sums = jnp.sum(weight * fresh * fresh, axis=0, keepdims=True)
        for j in range(8):
            dens[j : j + 1, i * 128 : (i + 1) * 128] = sums[:, j * 128 : (j + 1) * 128]
    block = dens[...].astype(bf16)
    for peer in range(PEERS):
        out_ref[peer * OWN : (peer + 1) * OWN, FULL:] = block


def share_kernel(meta, dens_ref, table_ref, out_ref, box):
    sx, sy, sz = box_size(meta)
    frag, band = meta[PLACE, 0], meta[PLACE, 1]
    groups = sy // 16
    lane = lax.broadcasted_iota(jnp.int32, (8, 128), 1)
    z = lane % BOX
    live = (z < sz).astype(f32)
    box[...] = jnp.zeros((BOX, 32, 128), f32)

    def tile(at):
        return dens_ref[at // 8, :, pl.ds(aligned(at % 8 * 128), 128)].astype(f32)

    def put(x, g, value):
        box[x, pl.ds(pl.multiple_of(g * 8, 8), 8), :] = value

    def parts(deep, body):
        @pl.when(sz == deep)
        def _():
            def outer(q, carry):
                def inner(g, c):
                    body(4 * q, g, [tile((q * groups + g) * (deep // 16) + p) for p in range(deep // 16)])
                    return c

                return lax.fori_loop(0, groups, inner, carry)

            lax.fori_loop(0, sx // 4, outer, 0)

    def whole(x, g, values):
        for p in range(4):
            put(x + p, g, values[p])

    def half(x, g, values):
        for p in range(2):
            put(x + 2 * p, g, values[p] * live)
            put(x + 2 * p + 1, g, pltpu.roll(values[p], 96, 1) * live)

    def most(x, g, values):
        gap = (z >= 48).astype(f32)
        for p in range(3):
            put(x + p, g, values[p] * live)
        rest = [pltpu.roll(values[p] * gap, 80 + 16 * p, 1) for p in range(3)]
        put(x + 3, g, rest[0] + rest[1] + rest[2])

    parts(64, whole)
    parts(32, half)
    parts(48, most)

    ox, oy, _ = box_offset(meta, frag)

    def plane(x):
        inside = ((x >= 0) & (x < sx)).astype(f32)
        return (box[jnp.clip(x, 0, BOX - 1)] * inside).astype(bf16)

    for i in range(4):
        value = plane(4 * band + i - ox)
        for other in range(8):
            out_ref[other, i * 32 : (i + 1) * 32, :] = value
    for other in range(8):
        for j in range(2):
            value = plane(box_offset(meta, other)[0] + 2 * band + j - ox)
            out_ref[other, (4 + j) * 32 : (5 + j) * 32, :] = value

    wide = lax.broadcasted_iota(jnp.int32, (32, 128), 1)
    even = table_ref[pl.ds(oy, 32, stride=2), :]
    odd = table_ref[pl.ds(oy + 1, 32, stride=2), :]
    weights = []
    for k in range(4):
        pick = wide == 4 * band + k
        first = jnp.sum(jnp.where(pick, even, 0.0), axis=1, keepdims=True)
        second = jnp.sum(jnp.where(pick, odd, 0.0), axis=1, keepdims=True)
        weights.append(jnp.where(wide < BOX, first, second))
    low = lane < BOX
    for pair in range(2):
        for part in range(4):
            rows = []
            for half in range(2):
                start = part * 16 + half * 8
                cube = box[start : start + 8]
                sums = []
                for k in (2 * pair, 2 * pair + 1):
                    s = jnp.sum(cube * weights[k][None], axis=1)
                    sums.append(s + pltpu.roll(s, BOX, 1))
                rows.append(jnp.where(low, sums[0], sums[1]))
            value = jnp.concatenate(rows, axis=0).astype(bf16)
            at = 192 + pair * BOX + part * 16
            for other in range(8):
                out_ref[other, at : at + 16, :] = value


def place_kernel(meta, in_ref, patched_ref, placed, target):
    lane = lax.broadcasted_iota(jnp.int32, (32, 128), 1)
    low = lane < BOX
    wide = lax.broadcasted_iota(jnp.int32, (BOX, G), 1)
    line = lax.broadcasted_iota(jnp.int32, (BOX, G), 0)
    for f in range(8):
        _, oy, oz = box_offset(meta, f)
        sign = meta[SIGNS, f].astype(f32)
        for i in range(6):
            value = in_ref[f, i * 32 : (i + 1) * 32, :].astype(f32)
            first = pltpu.roll(jnp.where(low, value, 0.0), oz, 1)
            second = pltpu.roll(jnp.where(low, 0.0, value), (oz + BOX) % G, 1)
            placed[f * BOX : f * BOX + 32, i * G : (i + 1) * G] = first.astype(bf16)
            placed[f * BOX + 32 : (f + 1) * BOX, i * G : (i + 1) * G] = second.astype(bf16)
        lands = oy + 2 * (line % 32) + line // 32
        target[f * BOX : (f + 1) * BOX, :] = jnp.where(wide == lands, sign, 0.0).astype(bf16)
    across = (((0,), (0,)), ((), ()))
    patched_ref[...] = lax.dot_general(target[...], placed[...], across, preferred_element_type=f32)


def solve_kernel(meta, in_ref, table_ref, column_ref, row_ref, out_ref, spread, along, cols, turned):
    frag, band = meta[PLACE, 0], meta[PLACE, 1]
    dot = functools.partial(lax.dot_general, preferred_element_type=f32)
    across = (((0,), (0,)), ((), ()))
    half = lax.broadcasted_iota(jnp.int32, (G, G), 1) < BOX
    for f in range(8):
        ox, _, oz = box_offset(meta, f)
        sign = meta[SIGNS, f].astype(f32)
        part = table_ref[pl.ds(oz, BOX), :]
        part = halves(jnp.concatenate([part, part], axis=0))
        value = in_ref[f, 192:320, :].astype(f32)
        both = jnp.concatenate([jnp.where(half, value, 0.0), jnp.where(half, 0.0, value)], axis=0).astype(bf16)
        both = jnp.dot(both, part[0], preferred_element_type=f32) + jnp.dot(both, part[1], preferred_element_type=f32)
        for parity in range(2):
            for pair in range(2):
                k = 2 * pair + parity
                at = parity * G + pair * BOX
                spread[f * BOX : (f + 1) * BOX, k * G : (k + 1) * G] = both[at : at + BOX, :]
        along[f * BOX : (f + 1) * BOX, :] = table_ref[pl.ds(ox, BOX), :] * sign
    left, right = halves(along[...]), halves(spread[...])
    spectrum = dot(left[0], right[0], across) + (dot(left[0], right[1], across) + dot(left[1], right[0], across))
    table = halves(table_ref[0:G, :])
    ex = column_ref[...]
    ez = row_ref[...]
    spot = lax.broadcasted_iota(jnp.int32, (1, G), 1)
    scaled = []
    for k in range(4):
        ey = jnp.sum(jnp.where(spot == 4 * band + k, ez, 0.0), axis=1, keepdims=True)
        scaled.append(spectrum[:, k * G : (k + 1) * G] * (screening / (ex + ey + ez + screening)))
    solved = product(table, halves(jnp.concatenate(scaled, axis=1)))
    for k in range(4):
        cols[k, 0:G, :] = product(halves(solved[:, k * G : (k + 1) * G]), table)
        cols[k, G : G + BOX, :] = jnp.zeros((BOX, G), f32)
    ox = box_offset(meta, frag)[0]
    for k in range(4):
        for i in range(6):
            part = cols[k, pl.ds(i, 32, stride=4), :] if i < 4 else cols[k, pl.ds(ox + i - 4, 32, stride=2), :]
            turned[i % 3, pl.ds(2 * k + i // 3, 32, stride=8), :] = part
    for i in range(3):
        out_ref[:, i * G : (i + 1) * G] = turned[i].astype(bf16)


def total_kernel(meta, in_ref, local_ref, table_ref, slab_ref, window_ref, columns, rows):
    sx, sy, sz = box_size(meta)
    frag, band = meta[PLACE, 0], meta[PLACE, 1]
    _, oy, oz = box_offset(meta, frag)
    table = halves(table_ref[0:G, :])
    for i in range(3):
        columns[i] = in_ref[:, i * G : (i + 1) * G].astype(f32)

    def total(i):
        part = columns[i % 3, pl.ds(i // 3, G, stride=2), :].astype(bf16)
        hartree = jnp.dot(table[0], part, preferred_element_type=f32) + jnp.dot(table[1], part, preferred_element_type=f32)
        return hartree - local_ref[:, i * G : (i + 1) * G]

    for i in range(4):
        slab_ref[i] = total(i)
    lane = lax.broadcasted_iota(jnp.int32, (32, 128), 1)
    line = lax.broadcasted_iota(jnp.int32, (32, 128), 0)
    live = ((lane % BOX < sz) & (2 * line + lane // BOX < sy)).astype(f32)
    low = lane < BOX
    for j in range(2):
        rows[0:G, :] = total(4 + j)
        rows[G : G + BOX, :] = jnp.zeros((BOX, G), f32)
        even = pltpu.roll(rows[pl.ds(oy, 32, stride=2), :], (G - oz) % G, 1)
        odd = pltpu.roll(rows[pl.ds(oy + 1, 32, stride=2), :], (G + BOX - oz) % G, 1)
        inside = (2 * band + j < sx).astype(f32)
        value = (jnp.where(low, even, odd) * live * inside).astype(bf16)
        for peer in range(PEERS):
            window_ref[peer, j * 32 : (j + 1) * 32, :] = value


def swap(block, axis="band"):
    return lax.all_to_all(block, axis, split_axis=0, concat_axis=0, tiled=True)


def swap_trial(volume, trial):
    lanes = volume * 128
    if lanes == FULL:
        return swap(trial)
    return jnp.pad(swap(trial[:, :, :lanes]), ((0, 0), (0, 0), (0, FULL - lanes)))


def swap_fresh(volume, block):
    lanes = volume * 128
    if lanes == FULL:
        return swap(block)
    tiles = -(-volume // OWN)
    width = tiles * 128
    back = swap(jnp.concatenate([block[:, :, :lanes], block[:, :, FULL : FULL + width]], axis=2))
    dens = back[:, :, lanes:].reshape(PEERS, OWN, tiles, 128).transpose(0, 2, 1, 3).reshape(PEERS, OWN * width)
    dens = jnp.pad(dens[:, :lanes].reshape(PEERS * lanes), (0, CELLS - PEERS * lanes))
    dens = dens.reshape(PEERS, OWN, OWN, 128).transpose(0, 2, 1, 3).reshape(PEERS, OWN, EXTRA)
    return jnp.concatenate([jnp.pad(back[:, :, :lanes], ((0, 0), (0, 0), (0, FULL - lanes))), dens], axis=2)


def body(wave_coeffs, old_potential, occupations, box_sizes, box_offsets, patch_signs):
    fragment = lax.axis_index("frag")
    band_index = lax.axis_index("band")
    here = jnp.where(jnp.arange(8) == 0, fragment, band_index).astype(jnp.int32)
    meta = jnp.concatenate([box_sizes.T, box_offsets.T, patch_signs[None], here[None]], axis=0)
    padded, eigen = sine_table()
    table = jnp.asarray(padded)
    eigen_row, eigen_column = jnp.asarray(eigen[None, :]), jnp.asarray(eigen[:, None])

    trial, kind = pl.pallas_call(
        trial_kernel,
        out_shape=(jax.ShapeDtypeStruct((PEERS, OWN, FULL), bf16), jax.ShapeDtypeStruct((1,), jnp.int32)),
        in_specs=[smem(), pl.BlockSpec(memory_space=pltpu.HBM), pl.BlockSpec(memory_space=pltpu.HBM)],
        out_specs=(vmem(), smem()),
        scratch_shapes=[
            pltpu.VMEM((OWN, 4096), f32),
            pltpu.VMEM((OWN, CELLS), bf16),
            pltpu.VMEM((1, CELLS), f32),
            pltpu.SemaphoreType.DMA((2, BOX // 4)),
        ],
        compiler_params=params(56),
        name="trial",
    )(meta, wave_coeffs[0], old_potential)
    kind = kind[0]
    rows = lax.switch(kind, [functools.partial(swap_trial, v) for v in VOLUMES], trial)
    rows = rows.reshape(NB, FULL)
    partial_value = pl.pallas_call(
        gram_kernel,
        out_shape=jax.ShapeDtypeStruct((NB, NB), f32),
        in_specs=[pl.BlockSpec(memory_space=pltpu.HBM)],
        out_specs=vmem(),
        scratch_shapes=[pltpu.VMEM((OWN, NB, EXTRA), bf16), pltpu.SemaphoreType.DMA((OWN,))],
        compiler_params=params(32),
        name="gram",
    )(rows)
    share = swap(partial_value.reshape(PEERS, OWN, NB)).sum(axis=0)
    gram = swap(jnp.broadcast_to(share[None], (PEERS, OWN, NB))).reshape(NB, NB)
    coeff = pl.pallas_call(
        newton_kernel,
        out_shape=jax.ShapeDtypeStruct((NB, NB), bf16),
        in_specs=[vmem()],
        out_specs=vmem(),
        compiler_params=params(32),
        name="newton",
    )(gram)
    fresh = pl.pallas_call(
        fresh_kernel,
        out_shape=jax.ShapeDtypeStruct((NB, FULL + EXTRA), bf16),
        in_specs=[vmem(), pl.BlockSpec(memory_space=pltpu.HBM), vmem()],
        out_specs=vmem(),
        scratch_shapes=[
            pltpu.VMEM((OWN, NB, EXTRA), bf16),
            pltpu.SemaphoreType.DMA((OWN,)),
            pltpu.VMEM((OWN, EXTRA), f32),
        ],
        compiler_params=params(32),
        name="fresh",
    )(coeff, rows, occupations)
    fresh = fresh.reshape(PEERS, OWN, FULL + EXTRA)
    back = lax.switch(kind, [functools.partial(swap_fresh, v) for v in VOLUMES], fresh)
    shared = pl.pallas_call(
        share_kernel,
        out_shape=jax.ShapeDtypeStruct((8, 320, 128), bf16),
        grid=(1,),
        in_specs=[
            smem(),
            pl.BlockSpec((PEERS, OWN, EXTRA), lambda i: (0, 0, FULL // EXTRA)),
            pl.BlockSpec((G + BOX, G), lambda i: (0, 0)),
        ],
        out_specs=pl.BlockSpec((8, 320, 128), lambda i: (0, 0, 0)),
        scratch_shapes=[pltpu.VMEM((BOX, 32, 128), f32)],
        compiler_params=params(32),
        name="share",
    )(meta, back, table)
    parts = swap(shared, "frag")
    columns = pl.pallas_call(
        solve_kernel,
        out_shape=jax.ShapeDtypeStruct((2 * G, 3 * G), bf16),
        in_specs=[smem(), vmem(), vmem(), vmem(), vmem()],
        out_specs=vmem(),
        scratch_shapes=[
            pltpu.VMEM((8 * BOX, 4 * G), f32),
            pltpu.VMEM((8 * BOX, G), f32),
            pltpu.VMEM((4, G + BOX, G), f32),
            pltpu.VMEM((3, 2 * G, G), f32),
        ],
        compiler_params=params(32),
        name="solve",
    )(meta, parts, table, eigen_column, eigen_row)
    patched = pl.pallas_call(
        place_kernel,
        out_shape=jax.ShapeDtypeStruct((G, 6 * G), f32),
        in_specs=[smem(), vmem()],
        out_specs=vmem(),
        scratch_shapes=[pltpu.VMEM((8 * BOX, 6 * G), bf16), pltpu.VMEM((8 * BOX, G), bf16)],
        compiler_params=params(32),
        cost_estimate=pl.CostEstimate(flops=2 * 8 * BOX * 6 * G * G, bytes_accessed=2**20, transcendentals=0),
        name="place",
    )(meta, parts)
    columns = swap(columns.reshape(PEERS, 8, 3 * G)).reshape(2 * G, 3 * G)
    local = local_factor * jnp.cbrt(jnp.maximum(patched, 0.0))
    total_potential, window = pl.pallas_call(
        total_kernel,
        out_shape=(jax.ShapeDtypeStruct((4, G, G), f32), jax.ShapeDtypeStruct((PEERS, 64, 128), bf16)),
        in_specs=[smem(), vmem(), vmem(), vmem()],
        out_specs=(vmem(), vmem()),
        scratch_shapes=[pltpu.VMEM((3, 2 * G, G), f32), pltpu.VMEM((G + BOX, G), f32)],
        compiler_params=params(32),
        name="total",
    )(meta, columns, local, table)
    window = swap(window)
    waves_out = pl.pallas_call(
        unpack_kernel,
        out_shape=jax.ShapeDtypeStruct((OWN, CELLS), bf16),
        in_specs=[smem(), vmem()],
        out_specs=vmem(),
        compiler_params=params(32),
        name="unpack",
    )(meta, back)
    box_potential = window.astype(f32).reshape(1, CELLS)
    return (waves_out[None], box_potential, total_potential)


def solution(mesh):
    placed = (P("frag", "band", None), P("frag", None), P("frag", None), P(), P(), P())
    return jax.shard_map(
        body,
        mesh=mesh,
        in_specs=placed,
        out_specs=(P("frag", "band", None), P("frag", None), P("band", None, None)),
        check_vma=False,
    )
```

profile of v0, /device:TPU:32, one launch (start us, length us, event | category | flops | bytes accessed | tf_op | source)
XLA Modules:
  0.0 255.2 jit_solution(2026878559680161700)
XLA Ops:
  0.6 1.3 pad_add_fusion.meta
  2.0 9.6 %trial.1 = (bf16[32,8,8192]{2,1,0:T(8,128)(2,1)S(1)}, s32[1]{0:T(128)}) custom-call(s32[8,8]{1,0:T(8,128)} %pad_add_fusion.meta, bf16[8,262144]{1,0:T(8,128)(2,1)} %bitcast.144, f32[1,262144]{1,0:T(1,128)} %pot_in.1), custom_call_target="tpu_custom_call" | custom-call | tf_op jit(solution)/shard_map/trial/pallas_call | solution.py:566
  12.2 70.2 %conditional.2 = (bf16[256,8192]{1,0:T(8,128)(2,1)}) conditional(s32[]{:T(128)} %bitcast.92, bf16[32,8,8192]{2,1,0:T(8,128)(2,1)S(1)} %get-tuple-element.53, bf16[32,8,8192]{2,1,0:T(8,128)(2,1)S(1)} %get-tuple-element.53, bf16[32,8,8192]{2,1,0:T(8,128)(2,1)S(1)} %get-tuple-element.53, ...), branch_computations={%region_0.1_spmd, %region_1.2_spmd, %region_2.3_spmd, %region_3.4_... | conditional | bytes 19922952 | solution.py:581
  12.3 70.2 %all_to_all.114 = bf16[32,8,8192]{2,1,0:T(8,128)(2,1)} all-to-all(bf16[32,8,8192]{2,1,0:T(8,128)(2,1)S(1)} %param.9), channel_id=1, replica_groups=mesh['frag'=8,'band'=32] {'band'}, dimensions={0} | all-to-all | bytes 8388608 | tf_op jit(solution)/shard_map/cond/branch_9_fun/all_to_all | solution.py:534
  82.4 0.0 copy-start.3
  82.4 4.2 %gram.1 = f32[256,256]{1,0:T(8,128)S(1)} custom-call(bf16[256,8192]{1,0:T(8,128)(2,1)} %get-tuple-element.56.rows_ref), custom_call_target="tpu_custom_call" | custom-call | tf_op jit(solution)/shard_map/gram/pallas_call | solution.py:583
  86.6 19.0 %all_to_all.125 = f32[32,8,256]{2,1,0:T(8,128)S(1)} all-to-all(f32[32,8,256]{2,1,0:T(8,128)S(1)} %bitcast.130), channel_id=1, replica_groups=mesh['frag'=8,'band'=32] {'band'}, dimensions={0} | all-to-all | bytes 524288 | tf_op jit(solution)/shard_map/all_to_all | solution.py:534
  105.7 16.9 %all_to_all.126 = f32[32,8,256]{2,1,0:T(8,128)S(1)} all-to-all(f32[32,8,256]{2,1,0:T(8,128)S(1)} %broadcast_in_dim.24), channel_id=1, replica_groups=mesh['frag'=8,'band'=32] {'band'}, dimensions={0} | all-to-all | bytes 524288 | tf_op jit(solution)/shard_map/all_to_all | solution.py:534
  122.6 5.0 %newton.1.coeff_ref = bf16[256,256]{1,0:T(8,128)(2,1)S(1)} custom-call(f32[256,256]{1,0:T(8,128)S(1)} %bitcast.131), custom_call_target="tpu_custom_call" | custom-call | tf_op jit(solution)/shard_map/newton/pallas_call | solution.py:594
  127.6 0.0 copy-done.3
  127.6 3.7 %fresh.1 = bf16[256,9216]{1,0:T(8,128)(2,1)S(1)} custom-call(bf16[256,256]{1,0:T(8,128)(2,1)S(1)} %newton.1.coeff_ref, bf16[256,8192]{1,0:T(8,128)(2,1)} %get-tuple-element.56.rows_ref, f32[1,256]{1,0:T(1,128)S(1)} %copy-done.3), custom_call_target="tpu_custom_call" | custom-call | tf_op jit(solution)/shard_map/fresh/pallas_call | solution.py:602
  131.3 0.0 copy-start
  131.3 0.0 copy-start.1
  131.4 62.8 %conditional.3 = (bf16[32,8,9216]{2,1,0:T(8,128)(2,1)}) conditional(s32[]{:T(128)} %bitcast.92, bf16[32,8,9216]{2,1,0:T(8,128)(2,1)S(1)} %bitcast.133, bf16[32,8,9216]{2,1,0:T(8,128)(2,1)S(1)} %bitcast.134, bf16[32,8,9216]{2,1,0:T(8,128)(2,1)S(1)} %bitcast.135, bf16[32,8,9216]{2,1,0:T(8,128)(2,1)S(1)} %bitcast.136, ...), branch_computations={%region_11.12_spmd, %region_12.13_spmd, %region_13.14_spmd, %regio... | conditional | flops 21233664 | bytes 37617672 | solution.py:616
  131.4 62.7 %all_to_all.124 = bf16[32,8,9216]{2,1,0:T(8,128)(2,1)} all-to-all(bf16[32,8,9216]{2,1,0:T(8,128)(2,1)S(1)} %param.19), channel_id=1, replica_groups=mesh['frag'=8,'band'=32] {'band'}, dimensions={0} | all-to-all | bytes 9437184 | tf_op jit(solution)/shard_map/cond/branch_9_fun/all_to_all | solution.py:534
  194.1 0.0 copy-start.2
  194.1 0.0 copy-done
  194.2 0.0 copy-done.1
  194.2 4.0 %share.1 = bf16[8,320,128]{2,1,0:T(8,128)(2,1)S(1)} custom-call(s32[8,8]{1,0:T(8,128)S(1)} %copy-done.1, bf16[32,8,9216]{2,1,0:T(8,128)(2,1)} %get-tuple-element.57.in_ref.dens_ref, f32[192,128]{1,0:T(8,128)S(1)} %copy-done), custom_call_target="tpu_custom_call" | custom-call | tf_op jit(solution)/shard_map/share/pallas_call | solution.py:617
  198.2 14.2 %all_to_all.127.in_ref = bf16[8,320,128]{2,1,0:T(8,128)(2,1)S(1)} all-to-all(bf16[8,320,128]{2,1,0:T(8,128)(2,1)S(1)} %share.1), channel_id=1, replica_groups=mesh['frag'=8,'band'=32] {'frag'}, dimensions={0} | all-to-all | bytes 1310720 | tf_op jit(solution)/shard_map/all_to_all | solution.py:534
  212.4 0.0 copy-done.2
  212.4 0.0 copy-done.4
  212.4 2.6 %solve.1 = bf16[256,384]{1,0:T(8,128)(2,1)} custom-call(s32[8,8]{1,0:T(8,128)S(1)} %copy-done.1, bf16[8,320,128]{2,1,0:T(8,128)(2,1)S(1)} %all_to_all.127.in_ref, f32[192,128]{1,0:T(8,128)S(1)} %copy-done, f32[128,1]{1,0:T(8,128)S(1)} %copy-done.2, f32[1,128]{1,0:T(1,128)S(1)} %copy-done.4), custom_call_target="tpu_custom_call" | custom-call | tf_op jit(solution)/shard_map/solve/pallas_call | solution.py:632
  215.0 5.0 %all-to-all-start.23 = ((bf16[32,8,384]{2,1,0:T(8,128)(2,1)}), bf16[32,8,384]{2,1,0:T(8,128)(2,1)S(1)}, u32[]{:S(2)}, u32[]{:S(2)}) async-start(bf16[32,8,384]{2,1,0:T(8,128)(2,1)} %bitcast.97), calls=%async_computation.23 | async-start | bytes 393216 | tf_op jit(solution)/shard_map/all_to_all | solution.py:534
  220.0 1.2 place.1
  221.1 0.3 cbrt_multiply_fusion.local_ref
  221.5 9.3 %all-to-all-done.23 = bf16[32,8,384]{2,1,0:T(8,128)(2,1)S(1)} async-done(((bf16[32,8,384]{2,1,0:T(8,128)(2,1)}), bf16[32,8,384]{2,1,0:T(8,128)(2,1)S(1)}, u32[]{:S(2)}, u32[]{:S(2)}) %all-to-all-start.23) | async-done | bytes 196640 | tf_op jit(solution)/shard_map/all_to_all | solution.py:534
  230.8 1.8 total.1
  232.6 4.5 %all-to-all-start.24 = ((bf16[32,64,128]{2,1,0:T(8,128)(2,1)}), bf16[32,64,128]{2,1,0:T(8,128)(2,1)S(1)}, u32[]{:S(2)}, u32[]{:S(2)}) async-start(bf16[32,64,128]{2,1,0:T(8,128)(2,1)} %get-tuple-element.54), calls=%async_computation.24 | async-start | bytes 1048576 | tf_op jit(solution)/shard_map/all_to_all | solution.py:534
  237.0 6.7 %unpack.1 = bf16[8,262144]{1,0:T(8,128)(2,1)} custom-call(s32[8,8]{1,0:T(8,128)S(1)} %copy-done.1, bf16[32,8,9216]{2,1,0:T(8,128)(2,1)} %get-tuple-element.57.in_ref.dens_ref), custom_call_target="tpu_custom_call" | custom-call | tf_op jit(solution)/shard_map/unpack/pallas_call | solution.py:668
  243.7 10.4 %all-to-all-done.24 = bf16[32,64,128]{2,1,0:T(8,128)(2,1)S(1)} async-done(((bf16[32,64,128]{2,1,0:T(8,128)(2,1)}), bf16[32,64,128]{2,1,0:T(8,128)(2,1)S(1)}, u32[]{:S(2)}, u32[]{:S(2)}) %all-to-all-start.24) | async-done | bytes 524320 | tf_op jit(solution)/shard_map/all_to_all | solution.py:534
  254.1 1.1 reshape.216
  (4 shorter events, 0.1 us)
Async XLA Ops:
  82.4 45.2 %copy-start.3 = (f32[1,256]{1,0:T(1,128)S(1)}, f32[1,256]{1,0:T(1,128)}, u32[]{:S(2)}) copy-start(f32[1,256]{1,0:T(1,128)} %occ_ref.1) | copy-start | bytes 3076
  131.3 62.8 %copy-start = (f32[192,128]{1,0:T(8,128)S(1)}, f32[192,128]{1,0:T(8,128)}, u32[]{:S(2)}) copy-start(f32[192,128]{1,0:T(8,128)} %constant.82.clone.table_ref) | copy-start | bytes 294916
  131.3 62.8 %copy-start.1 = (s32[8,8]{1,0:T(8,128)S(1)}, s32[8,8]{1,0:T(8,128)}, u32[]{:S(2)}) copy-start(s32[8,8]{1,0:T(8,128)} %pad_add_fusion.meta) | copy-start | bytes 772
  194.1 18.3 %copy-start.2 = (f32[128,1]{1,0:T(8,128)S(1)}, f32[128,1]{1,0:T(8,128)}, u32[]{:S(2)}) copy-start(f32[128,1]{1,0:T(8,128)} %constant.84.clone.column_ref) | copy-start | bytes 1540
  194.1 18.3 %copy-start.4 = (f32[1,128]{1,0:T(1,128)S(1)}, f32[1,128]{1,0:T(1,128)}, u32[]{:S(2)}) copy-start(f32[1,128]{1,0:T(1,128)} %constant.83.clone.row_ref) | copy-start | bytes 1540
  215.0 15.8 %all-to-all-start.23 = ((bf16[32,8,384]{2,1,0:T(8,128)(2,1)}), bf16[32,8,384]{2,1,0:T(8,128)(2,1)S(1)}, u32[]{:S(2)}, u32[]{:S(2)}) async-start(bf16[32,8,384]{2,1,0:T(8,128)(2,1)} %bitcast.97), calls=%async_computation.23 | async-start | bytes 393216 | tf_op jit(solution)/shard_map/all_to_all | solution.py:534
  232.6 21.5 %all-to-all-start.24 = ((bf16[32,64,128]{2,1,0:T(8,128)(2,1)}), bf16[32,64,128]{2,1,0:T(8,128)(2,1)S(1)}, u32[]{:S(2)}, u32[]{:S(2)}) async-start(bf16[32,64,128]{2,1,0:T(8,128)(2,1)} %get-tuple-element.54), calls=%async_computation.24 | async-start | bytes 1048576 | tf_op jit(solution)/shard_map/all_to_all | solution.py:534
where the time goes:
time: 256 us; the launch traced here: 255 us
  blocking collectives  183 us (71%)
  Pallas kernels  38.7 us (15%)
  waiting for transfers between devices  19.7 us (8%)
  starting transfers between devices  9.44 us (4%)
  other arithmetic  2.77 us (1%)
    all_to_all x5, blocking collectives, swap(): return lax.all_to_all(block, axis, split_axis=0, concat_axis=0, tiled=True)  183 us
    all_to_all x2, waiting for transfers between devices, swap(): return lax.all_to_all(block, axis, split_axis=0, concat_axis=0, tiled=True)  19.7 us
    pallas_call x1, Pallas kernels, body(): pl.pallas_call(trial_kernel, out_shape=(jax.ShapeDtypeStruct((PEERS, OWN,...  9.58 us
    all_to_all x2, starting transfers between devices, swap(): return lax.all_to_all(block, axis, split_axis=0, concat_axis=0, tiled=True)  9.44 us
    pallas_call x1, Pallas kernels, body(): pl.pallas_call(unpack_kernel, out_shape=jax.ShapeDtypeStruct((OWN, CELLS)...  6.65 us
  transfers between devices with their start and end apart: 2, of which 2 were waited for; matrix products, arithmetic and copies ran while one was open for 0% of the time, Pallas kernels for 3%

commit v1 on v0

--- a/solution.py
+++ b/solution.py
@@ -285,16 +285,10 @@
         some(deep)
 
 
-def gram_kernel(rows_ref, out_ref, blocks, arrived):
-    copies = []
-    for i in range(OWN):
-        part = rows_ref.at[:, i * EXTRA : (i + 1) * EXTRA]
-        copies.append(pltpu.make_async_copy(part, blocks.at[i], arrived.at[i]))
-        copies[-1].start()
+def gram_kernel(rows_ref, out_ref):
     total = jnp.zeros((NB, NB), f32)
     for i in range(OWN):
-        copies[i].wait()
-        block = blocks[i]
+        block = rows_ref[:, i * EXTRA : (i + 1) * EXTRA]
         total = total + lax.dot_general(block, block, (((1,), (1,)), ((), ())), preferred_element_type=f32)
     out_ref[...] = total
 
@@ -329,17 +323,11 @@
     out_ref[...] = (inverse / jnp.sqrt(frobenius)).T.astype(bf16)
 
 
-def fresh_kernel(coeff_ref, rows_ref, occ_ref, out_ref, blocks, arrived, dens):
-    copies = []
-    for i in range(OWN):
-        part = rows_ref.at[:, i * EXTRA : (i + 1) * EXTRA]
-        copies.append(pltpu.make_async_copy(part, blocks.at[i], arrived.at[i]))
-        copies[-1].start()
+def fresh_kernel(coeff_ref, rows_ref, occ_ref, out_ref, dens):
     weight = jnp.broadcast_to(occ_ref[...] * (1.0 / NB), (128, NB)).T[:, 0:1]
     coeff = coeff_ref[...]
     for i in range(OWN):
-        copies[i].wait()
-        fresh = jnp.dot(coeff, blocks[i], preferred_element_type=f32)
+        fresh = jnp.dot(coeff, rows_ref[:, i * EXTRA : (i + 1) * EXTRA], preferred_element_type=f32)
         out_ref[:, i * EXTRA : (i + 1) * EXTRA] = fresh.astype(bf16)
         sums = jnp.sum(weight * fresh * fresh, axis=0, keepdims=True)
         for j in range(8):
@@ -583,10 +571,9 @@
     partial_value = pl.pallas_call(
         gram_kernel,
         out_shape=jax.ShapeDtypeStruct((NB, NB), f32),
-        in_specs=[pl.BlockSpec(memory_space=pltpu.HBM)],
+        in_specs=[vmem()],
         out_specs=vmem(),
-        scratch_shapes=[pltpu.VMEM((OWN, NB, EXTRA), bf16), pltpu.SemaphoreType.DMA((OWN,))],
-        compiler_params=params(32),
+        compiler_params=params(16),
         name="gram",
     )(rows)
     share = swap(partial_value.reshape(PEERS, OWN, NB)).sum(axis=0)
@@ -596,20 +583,16 @@
         out_shape=jax.ShapeDtypeStruct((NB, NB), bf16),
         in_specs=[vmem()],
         out_specs=vmem(),
-        compiler_params=params(32),
+        compiler_params=params(16),
         name="newton",
     )(gram)
     fresh = pl.pallas_call(
         fresh_kernel,
         out_shape=jax.ShapeDtypeStruct((NB, FULL + EXTRA), bf16),
-        in_specs=[vmem(), pl.BlockSpec(memory_space=pltpu.HBM), vmem()],
+        in_specs=[vmem(), vmem(), vmem()],
         out_specs=vmem(),
-        scratch_shapes=[
-            pltpu.VMEM((OWN, NB, EXTRA), bf16),
-            pltpu.SemaphoreType.DMA((OWN,)),
-            pltpu.VMEM((OWN, EXTRA), f32),
-        ],
-        compiler_params=params(32),
+        scratch_shapes=[pltpu.VMEM((OWN, EXTRA), f32)],
+        compiler_params=params(16),
         name="fresh",
     )(coeff, rows, occupations)
     fresh = fresh.reshape(PEERS, OWN, FULL + EXTRA)

time: 256 us -> 254 us (level)
  no operation moved by 1% of the time
where the time goes in v1:
time: 254 us; the launch traced here: 253 us
  blocking collectives  182 us (72%)
  Pallas kernels  38.1 us (15%)
  waiting for transfers between devices  19.6 us (8%)
  starting transfers between devices  9.44 us (4%)
  other arithmetic  2.77 us (1%)
    all_to_all x5, blocking collectives, swap(): return lax.all_to_all(block, axis, split_axis=0, concat_axis=0, tiled=True)  182 us
    all_to_all x2, waiting for transfers between devices, swap(): return lax.all_to_all(block, axis, split_axis=0, concat_axis=0, tiled=True)  19.6 us
    pallas_call x1, Pallas kernels, body(): pl.pallas_call(trial_kernel, out_shape=(jax.ShapeDtypeStruct((PEERS, OWN,...  9.55 us
    all_to_all x2, starting transfers between devices, swap(): return lax.all_to_all(block, axis, split_axis=0, concat_axis=0, tiled=True)  9.44 us
    pallas_call x1, Pallas kernels, body(): pl.pallas_call(unpack_kernel, out_shape=jax.ShapeDtypeStruct((OWN, CELLS)...  6.65 us
  transfers between devices with their start and end apart: 2, of which 2 were waited for; matrix products, arithmetic and copies ran while one was open for 0% of the time, Pallas kernels for 3%

profile of v1, /device:TPU:32, one launch (start us, length us, event | category | flops | bytes accessed | tf_op | source)
XLA Modules:
  0.0 253.1 jit_solution(7503310401469544165)
XLA Ops:
  0.6 1.3 pad_add_fusion.meta
  2.0 9.6 %trial.1 = (bf16[32,8,8192]{2,1,0:T(8,128)(2,1)S(1)}, s32[1]{0:T(128)}) custom-call(s32[8,8]{1,0:T(8,128)} %pad_add_fusion.meta, bf16[8,262144]{1,0:T(8,128)(2,1)} %bitcast.144, f32[1,262144]{1,0:T(1,128)} %pot_in.1), custom_call_target="tpu_custom_call" | custom-call | tf_op jit(solution)/shard_map/trial/pallas_call | solution.py:554
  12.2 70.4 %conditional.2 = (bf16[256,8192]{1,0:T(8,128)(2,1)}) conditional(s32[]{:T(128)} %bitcast.92, bf16[32,8,8192]{2,1,0:T(8,128)(2,1)S(1)} %get-tuple-element.53, bf16[32,8,8192]{2,1,0:T(8,128)(2,1)S(1)} %get-tuple-element.53, bf16[32,8,8192]{2,1,0:T(8,128)(2,1)S(1)} %get-tuple-element.53, ...), branch_computations={%region_0.1_spmd, %region_1.2_spmd, %region_2.3_spmd, %region_3.4_... | conditional | bytes 19922952 | solution.py:569
  12.2 70.3 %all_to_all.114 = bf16[32,8,8192]{2,1,0:T(8,128)(2,1)} all-to-all(bf16[32,8,8192]{2,1,0:T(8,128)(2,1)S(1)} %param.9), channel_id=1, replica_groups=mesh['frag'=8,'band'=32] {'band'}, dimensions={0} | all-to-all | bytes 8388608 | tf_op jit(solution)/shard_map/cond/branch_9_fun/all_to_all | solution.py:522
  82.5 0.0 copy-start.3
  82.5 3.5 %gram.1 = f32[256,256]{1,0:T(8,128)S(1)} custom-call(bf16[256,8192]{1,0:T(8,128)(2,1)} %get-tuple-element.56.rows_ref), custom_call_target="tpu_custom_call" | custom-call | tf_op jit(solution)/shard_map/gram/pallas_call | solution.py:571
  86.0 18.3 %all_to_all.125 = f32[32,8,256]{2,1,0:T(8,128)S(1)} all-to-all(f32[32,8,256]{2,1,0:T(8,128)S(1)} %bitcast.130), channel_id=1, replica_groups=mesh['frag'=8,'band'=32] {'band'}, dimensions={0} | all-to-all | bytes 524288 | tf_op jit(solution)/shard_map/all_to_all | solution.py:522
  104.4 16.2 %all_to_all.126 = f32[32,8,256]{2,1,0:T(8,128)S(1)} all-to-all(f32[32,8,256]{2,1,0:T(8,128)S(1)} %broadcast_in_dim.24), channel_id=1, replica_groups=mesh['frag'=8,'band'=32] {'band'}, dimensions={0} | all-to-all | bytes 524288 | tf_op jit(solution)/shard_map/all_to_all | solution.py:522
  120.6 5.0 %newton.1.coeff_ref = bf16[256,256]{1,0:T(8,128)(2,1)S(1)} custom-call(f32[256,256]{1,0:T(8,128)S(1)} %bitcast.131), custom_call_target="tpu_custom_call" | custom-call | tf_op jit(solution)/shard_map/newton/pallas_call | solution.py:581
  125.6 0.0 copy-done.3
  125.6 3.7 %fresh.1 = bf16[256,9216]{1,0:T(8,128)(2,1)S(1)} custom-call(bf16[256,256]{1,0:T(8,128)(2,1)S(1)} %newton.1.coeff_ref, bf16[256,8192]{1,0:T(8,128)(2,1)} %get-tuple-element.56.rows_ref, f32[1,256]{1,0:T(1,128)S(1)} %copy-done.3), custom_call_target="tpu_custom_call" | custom-call | tf_op jit(solution)/shard_map/fresh/pallas_call | solution.py:589
  129.3 0.0 copy-start
  129.4 0.0 copy-start.1
  129.4 62.8 %conditional.3 = (bf16[32,8,9216]{2,1,0:T(8,128)(2,1)}) conditional(s32[]{:T(128)} %bitcast.92, bf16[32,8,9216]{2,1,0:T(8,128)(2,1)S(1)} %bitcast.133, bf16[32,8,9216]{2,1,0:T(8,128)(2,1)S(1)} %bitcast.134, bf16[32,8,9216]{2,1,0:T(8,128)(2,1)S(1)} %bitcast.135, bf16[32,8,9216]{2,1,0:T(8,128)(2,1)S(1)} %bitcast.136, ...), branch_computations={%region_11.12_spmd, %region_12.13_spmd, %region_13.14_spmd, %regio... | conditional | flops 21233664 | bytes 60031064 | solution.py:599
  129.4 62.7 %all_to_all.124 = bf16[32,8,9216]{2,1,0:T(8,128)(2,1)} all-to-all(bf16[32,8,9216]{2,1,0:T(8,128)(2,1)S(1)} %param.19), channel_id=1, replica_groups=mesh['frag'=8,'band'=32] {'band'}, dimensions={0} | all-to-all | bytes 9437184 | tf_op jit(solution)/shard_map/cond/branch_9_fun/all_to_all | solution.py:522
  192.2 0.0 copy-start.2
  192.2 0.0 copy-done
  192.2 0.0 copy-done.1
  192.2 4.1 %share.1 = bf16[8,320,128]{2,1,0:T(8,128)(2,1)S(1)} custom-call(s32[8,8]{1,0:T(8,128)S(1)} %copy-done.1, bf16[32,8,9216]{2,1,0:T(8,128)(2,1)} %get-tuple-element.57.in_ref.dens_ref, f32[192,128]{1,0:T(8,128)S(1)} %copy-done), custom_call_target="tpu_custom_call" | custom-call | tf_op jit(solution)/shard_map/share/pallas_call | solution.py:600
  196.2 14.2 %all_to_all.127.in_ref = bf16[8,320,128]{2,1,0:T(8,128)(2,1)S(1)} all-to-all(bf16[8,320,128]{2,1,0:T(8,128)(2,1)S(1)} %share.1), channel_id=1, replica_groups=mesh['frag'=8,'band'=32] {'frag'}, dimensions={0} | all-to-all | bytes 1310720 | tf_op jit(solution)/shard_map/all_to_all | solution.py:522
  210.4 0.0 copy-done.2
  210.4 0.0 copy-done.4
  210.4 2.6 %solve.1 = bf16[256,384]{1,0:T(8,128)(2,1)} custom-call(s32[8,8]{1,0:T(8,128)S(1)} %copy-done.1, bf16[8,320,128]{2,1,0:T(8,128)(2,1)S(1)} %all_to_all.127.in_ref, f32[192,128]{1,0:T(8,128)S(1)} %copy-done, f32[128,1]{1,0:T(8,128)S(1)} %copy-done.2, f32[1,128]{1,0:T(1,128)S(1)} %copy-done.4), custom_call_target="tpu_custom_call" | custom-call | tf_op jit(solution)/shard_map/solve/pallas_call | solution.py:615
  213.0 5.0 %all-to-all-start.23 = ((bf16[32,8,384]{2,1,0:T(8,128)(2,1)}), bf16[32,8,384]{2,1,0:T(8,128)(2,1)S(1)}, u32[]{:S(2)}, u32[]{:S(2)}) async-start(bf16[32,8,384]{2,1,0:T(8,128)(2,1)} %bitcast.97), calls=%async_computation.23 | async-start | bytes 393216 | tf_op jit(solution)/shard_map/all_to_all | solution.py:522
  218.0 1.2 place.1
  219.2 0.3 cbrt_multiply_fusion.local_ref
  219.5 9.3 %all-to-all-done.23 = bf16[32,8,384]{2,1,0:T(8,128)(2,1)S(1)} async-done(((bf16[32,8,384]{2,1,0:T(8,128)(2,1)}), bf16[32,8,384]{2,1,0:T(8,128)(2,1)S(1)}, u32[]{:S(2)}, u32[]{:S(2)}) %all-to-all-start.23) | async-done | bytes 196640 | tf_op jit(solution)/shard_map/all_to_all | solution.py:522
  228.8 1.8 total.1
  230.6 4.5 %all-to-all-start.24 = ((bf16[32,64,128]{2,1,0:T(8,128)(2,1)}), bf16[32,64,128]{2,1,0:T(8,128)(2,1)S(1)}, u32[]{:S(2)}, u32[]{:S(2)}) async-start(bf16[32,64,128]{2,1,0:T(8,128)(2,1)} %get-tuple-element.54), calls=%async_computation.24 | async-start | bytes 1048576 | tf_op jit(solution)/shard_map/all_to_all | solution.py:522
  235.1 6.7 %unpack.1 = bf16[8,262144]{1,0:T(8,128)(2,1)} custom-call(s32[8,8]{1,0:T(8,128)S(1)} %copy-done.1, bf16[32,8,9216]{2,1,0:T(8,128)(2,1)} %get-tuple-element.57.in_ref.dens_ref), custom_call_target="tpu_custom_call" | custom-call | tf_op jit(solution)/shard_map/unpack/pallas_call | solution.py:651
  241.7 10.3 %all-to-all-done.24 = bf16[32,64,128]{2,1,0:T(8,128)(2,1)S(1)} async-done(((bf16[32,64,128]{2,1,0:T(8,128)(2,1)}), bf16[32,64,128]{2,1,0:T(8,128)(2,1)S(1)}, u32[]{:S(2)}, u32[]{:S(2)}) %all-to-all-start.24) | async-done | bytes 524320 | tf_op jit(solution)/shard_map/all_to_all | solution.py:522
  252.0 1.1 reshape.216
  (4 shorter events, 0.1 us)
Async XLA Ops:
  82.5 43.1 %copy-start.3 = (f32[1,256]{1,0:T(1,128)S(1)}, f32[1,256]{1,0:T(1,128)}, u32[]{:S(2)}) copy-start(f32[1,256]{1,0:T(1,128)} %occ_ref.1) | copy-start | bytes 3076
  129.3 62.8 %copy-start = (f32[192,128]{1,0:T(8,128)S(1)}, f32[192,128]{1,0:T(8,128)}, u32[]{:S(2)}) copy-start(f32[192,128]{1,0:T(8,128)} %constant.82.clone.table_ref) | copy-start | bytes 294916
  129.4 62.8 %copy-start.1 = (s32[8,8]{1,0:T(8,128)S(1)}, s32[8,8]{1,0:T(8,128)}, u32[]{:S(2)}) copy-start(s32[8,8]{1,0:T(8,128)} %pad_add_fusion.meta) | copy-start | bytes 772
  192.2 18.3 %copy-start.2 = (f32[128,1]{1,0:T(8,128)S(1)}, f32[128,1]{1,0:T(8,128)}, u32[]{:S(2)}) copy-start(f32[128,1]{1,0:T(8,128)} %constant.84.clone.column_ref) | copy-start | bytes 1540
  192.2 18.3 %copy-start.4 = (f32[1,128]{1,0:T(1,128)S(1)}, f32[1,128]{1,0:T(1,128)}, u32[]{:S(2)}) copy-start(f32[1,128]{1,0:T(1,128)} %constant.83.clone.row_ref) | copy-start | bytes 1540
  213.0 15.8 %all-to-all-start.23 = ((bf16[32,8,384]{2,1,0:T(8,128)(2,1)}), bf16[32,8,384]{2,1,0:T(8,128)(2,1)S(1)}, u32[]{:S(2)}, u32[]{:S(2)}) async-start(bf16[32,8,384]{2,1,0:T(8,128)(2,1)} %bitcast.97), calls=%async_computation.23 | async-start | bytes 393216 | tf_op jit(solution)/shard_map/all_to_all | solution.py:522
  230.6 21.4 %all-to-all-start.24 = ((bf16[32,64,128]{2,1,0:T(8,128)(2,1)}), bf16[32,64,128]{2,1,0:T(8,128)(2,1)S(1)}, u32[]{:S(2)}, u32[]{:S(2)}) async-start(bf16[32,64,128]{2,1,0:T(8,128)(2,1)} %get-tuple-element.54), calls=%async_computation.24 | async-start | bytes 1048576 | tf_op jit(solution)/shard_map/all_to_all | solution.py:522
